TPU v7x, 32 devices: a whole 2x2x4 slice. The times are simulated.
32 devices in a mesh: groups: 2 (over y), expert: 4 (over x, core), replica: 4 (over z).
Axes of the slice: x: 2, y: 2, z: 4, core: 2. Of those that a mesh axis runs over, the one named last changes fastest.
Arguments:
- tokens: bfloat16 [768, 7168], P(('groups', 'expert'), 'replica'), parts along dimension 0, may hold values from -6 to 6
- expert_ids: int32 [768, 2], P(('groups', 'expert')), parts along dimension 0, may hold values from 0 to 3, all different within a row; in each aligned block of 96 rows (0 to 95, 96 to 191, ...) at most 60 rows name the same one
- affinity: float32 [768, 2], P(('groups', 'expert')), parts along dimension 0, may hold values from 0.05 to 1
- gate_up: bfloat16 [4, 7168, 2, 2048], P('expert', 'replica'), may hold values from -0.0625 to 0.0625
- down_proj: bfloat16 [4, 2048, 7168], P('expert', None, 'replica'), may hold values from -0.125 to 0.125
Outputs:
- mixed: bfloat16 [768, 7168], P(('groups', 'expert'), 'replica'), parts along dimension 0
There are 2 independent parts, one for each index of `groups`. A program takes and returns all parts, laid end to end along the dimension named above; an argument that names none is the same for every part. Nothing has to cross between parts.
Inputs may be any that keep to these rules, and one draw needn't show every extreme that they name: `expert_ids`: each row names 2 different experts. Within each aligned block of 96 rows no expert is named by more than 60 rows, a bound that some block reaches.
All inputs are finite; a program needn't handle non-finite values.
Results may differ from a plain program's by a relative error of at most 0.023.
Values may be sent and summed in bfloat16 or wider, within the bound.
A program may use at most 128 MiB of HBM per device.

v0:
```python
import jax
import jax.numpy as jnp
from jax import lax
from jax.sharding import PartitionSpec as P


def slot_table(expert_ids, expert_count, capacity):
    labels = lax.broadcasted_iota(jnp.int32, (1, 1, expert_count), 2)
    chosen = (expert_ids[:, :, None] == labels).astype(jnp.int32)
    per_row = jnp.sum(chosen, axis=1)
    before = jnp.cumsum(per_row, axis=0) - per_row
    slot_rank = jnp.sum(chosen * before[:, None, :], axis=2)
    return expert_ids * capacity + slot_rank


def per_device(tokens, expert_ids, affinity, gate_up, down_proj):
    expert_count = lax.axis_size("expert")
    row_count, top_count = expert_ids.shape
    capacity = 5 * row_count * top_count // (4 * expert_count)
    width_local = tokens.shape[1]
    hidden_width = down_proj.shape[1]
    slot_index = slot_table(expert_ids, expert_count, capacity)
    row_labels = jnp.broadcast_to(
        lax.broadcasted_iota(jnp.int32, (row_count, 1), 0), (row_count, top_count)
    )
    source = (
        jnp.full((expert_count * capacity,), row_count, jnp.int32)
        .at[slot_index.reshape(-1)]
        .set(row_labels.reshape(-1))
    )
    padded = jnp.concatenate([tokens, jnp.zeros((1, width_local), tokens.dtype)], axis=0)
    outgoing = padded[source].reshape(expert_count, capacity, width_local)
    pair_weight = gate_up[0].reshape(width_local, 2 * hidden_width)
    down_local = down_proj[0]
    slot_block = lax.all_to_all(outgoing, "expert", split_axis=0, concat_axis=0, tiled=True)
    group_count, item_count, feature_count = slot_block.shape
    partial_sum = jnp.dot(
        slot_block.reshape(group_count * item_count, feature_count),
        pair_weight,
        preferred_element_type=jnp.float32,
    )
    partial_rows = partial_sum.astype(jnp.bfloat16).reshape(
        group_count, item_count, 2, hidden_width
    )
    summed = lax.psum(partial_rows, "replica").astype(jnp.float32)
    hidden = (jax.nn.silu(summed[:, :, 0]) * summed[:, :, 1]).astype(jnp.bfloat16)
    result = jnp.dot(
        hidden.reshape(-1, hidden_width), down_local, preferred_element_type=jnp.float32
    )
    expert_rows = result.astype(jnp.bfloat16).reshape(expert_count, capacity, width_local)
    returned = lax.all_to_all(expert_rows, "expert", split_axis=0, concat_axis=0, tiled=True)
    picked = returned.reshape(expert_count * capacity, width_local)[slot_index]
    weights = 2.5 * affinity / jnp.sum(affinity, axis=1, keepdims=True)
    mixed = jnp.einsum("tk,tkd->td", weights, picked.astype(jnp.float32))
    return mixed.astype(jnp.bfloat16)


def solution(mesh):
    placed = (
        P(("groups", "expert"), "replica"),
        P(("groups", "expert"), None),
        P(("groups", "expert"), None),
        P("expert", "replica", None, None),
        P("expert", None, "replica"),
    )
    return jax.shard_map(
        per_device,
        mesh=mesh,
        in_specs=placed,
        out_specs=P(("groups", "expert"), "replica"),
        check_vma=False,
    )
```

profile of v0, /device:TPU:0, one launch (start us, length us, event | category | flops | bytes accessed | tf_op | source)
XLA Modules:
  0.0 176.7 jit_solution(14017311911551673025)
XLA Ops:
  6.5 0.7 convert_reduce_fusion
  7.2 0.1 copy.11
  7.3 0.1 reduce_window_sum.11
  7.5 0.7 select_reduce_fusion
  8.3 0.7 compare_select_fusion.1
  9.0 0.1 reshape.64
  9.2 0.1 reshape.91
  9.3 1.2 scatter_custom_fusion
  10.6 1.0 concatenate.3
  11.6 1.3 gather_fusion
  12.9 1.1 reshape.66
  14.0 4.2 %all-to-all-start = ((bf16[4,60,1792]{2,1,0:T(8,128)(2,1)}), bf16[4,60,1792]{2,1,0:T(8,128)(2,1)S(1)}, u32[]{:S(2)}, u32[]{:S(2)}) async-start(bf16[4,60,1792]{2,1,0:T(8,128)(2,1)} %reshape.66), calls=%async_computation | async-start | bytes 1835008 | tf_op jit(solution)/shard_map/all_to_all | solution.py:35
  18.2 16.1 %copy.19 = bf16[224,8,2,2048]{3,1,2,0:T(8,128)(2,1)} copy(bf16[224,8,2,2048]{3,2,1,0:T(2,128)(2,1)} %bitcast.21) | data formatting | bytes 29360128
  34.3 0.2 reshape.67
  34.5 10.3 %convolution_convert_fusion = bf16[240,4096]{1,0:T(8,128)(2,1)} fusion(bf16[240,1792]{1,0:T(8,128)(2,1)S(1)} %reshape.67, bf16[1792,4096]{1,0:T(8,128)(2,1)} %bitcast.22), kind=kOutput, calls=%fused_computation.5 | convolution fusion | flops 3524198400 | bytes 17506304 | tf_op jit(solution)/shard_map/dot_general | solution.py:37
  44.8 4.8 %reshape.68 = bf16[4,60,2,2048]{3,2,1,0:T(2,128)(2,1)S(1)} reshape(bf16[240,4096]{1,0:T(8,128)(2,1)} %convolution_convert_fusion) | data formatting | bytes 3932160 | tf_op jit(solution)/shard_map/reshape | solution.py:42
  49.7 2.1 %copy.15 = bf16[4,60,2,2048]{3,1,0,2:T(8,128)(2,1)} copy(bf16[4,60,2,2048]{3,2,1,0:T(2,128)(2,1)S(1)} %reshape.68) | data formatting | bytes 3932160 | tf_op jit(solution)/shard_map/reshape | solution.py:42
  51.8 89.2 %all-reduce.3.cloned.1.call-done = bf16[4,60,2,2048]{3,1,0,2:T(8,128)(2,1)} async-done(((bf16[4,60,2,2048]{3,1,0,2:T(8,128)(2,1)}), bf16[4,60,2,2048]{3,1,0,2:T(8,128)(2,1)}) %all-reduce.3.cloned.1.call-update) | async-done | bytes 1966096 | tf_op jit(solution)/shard_map/psum | solution.py:45
  141.0 2.1 %convert_element_type.25 = f32[4,60,2,2048]{3,1,0,2:T(8,128)S(1)} convert(bf16[4,60,2,2048]{3,1,0,2:T(8,128)(2,1)} %all-reduce.3.cloned.1.call-done) | non-fusion elementwise | flops 983040 | bytes 5898240 | tf_op jit(solution)/shard_map/convert_element_type | solution.py:45
  143.1 0.6 fusion.5
  143.8 0.2 convert_element_type.27
  144.0 5.0 %fusion.2 = bf16[240,1792]{1,0:T(8,128)(2,1)S(1)} fusion(bf16[240,2048]{1,0:T(8,128)(2,1)S(1)} %convert_element_type.27, bf16[1,2048,1792]{2,1,0:T(8,128)(2,1)} %param.9), kind=kOutput, calls=%fused_computation.6 | convolution fusion | flops 1762037760 | bytes 9183232 | tf_op jit(solution)/shard_map/dot_general | solution.py:47
  149.0 1.1 reshape.69
  150.1 3.5 %all-to-all-start.1 = ((bf16[4,60,1792]{2,1,0:T(8,128)(2,1)}), bf16[4,60,1792]{2,1,0:T(8,128)(2,1)S(1)}, u32[]{:S(2)}, u32[]{:S(2)}) async-start(bf16[4,60,1792]{2,1,0:T(8,128)(2,1)} %reshape.69), calls=%async_computation.1 | async-start | bytes 1835008 | tf_op jit(solution)/shard_map/all_to_all | solution.py:51
  153.7 0.1 reshape.81
  153.9 0.1 copy.17
  154.0 12.6 %all-to-all-done.1 = bf16[4,60,1792]{2,1,0:T(8,128)(2,1)S(1)} async-done(((bf16[4,60,1792]{2,1,0:T(8,128)(2,1)}), bf16[4,60,1792]{2,1,0:T(8,128)(2,1)S(1)}, u32[]{:S(2)}, u32[]{:S(2)}) %all-to-all-start.1) | async-done | bytes 860192 | tf_op jit(solution)/shard_map/all_to_all | solution.py:51
  166.6 0.2 reshape.70
  166.8 1.1 gather_fusion.1
  168.0 0.3 reshape.80
  168.2 0.9 fusion.8
  169.1 0.8 copy.21
  (16 shorter events, 0.4 us)
Async XLA Ops:
  14.0 20.3 %all-to-all-start = ((bf16[4,60,1792]{2,1,0:T(8,128)(2,1)}), bf16[4,60,1792]{2,1,0:T(8,128)(2,1)S(1)}, u32[]{:S(2)}, u32[]{:S(2)}) async-start(bf16[4,60,1792]{2,1,0:T(8,128)(2,1)} %reshape.66), calls=%async_computation | async-start | bytes 1835008 | tf_op jit(solution)/shard_map/all_to_all | solution.py:35
  18.2 122.8 %all-reduce.3.cloned.1.call-start = ((), (), s32[]{:S(2)}) async-start(), calls=%async_computation.2 | async-start | bytes 4194304 | tf_op jit(solution)/shard_map/psum | solution.py:45
  149.0 4.9 %copy-start = (f32[96,2]{0,1:T(2,128)S(1)}, f32[96,2]{0,1:T(2,128)}, u32[]{:S(2)}) copy-start(f32[96,2]{0,1:T(2,128)} %param.7) | copy-start | bytes 2308
  150.1 16.5 %all-to-all-start.1 = ((bf16[4,60,1792]{2,1,0:T(8,128)(2,1)}), bf16[4,60,1792]{2,1,0:T(8,128)(2,1)S(1)}, u32[]{:S(2)}, u32[]{:S(2)}) async-start(bf16[4,60,1792]{2,1,0:T(8,128)(2,1)} %reshape.69), calls=%async_computation.1 | async-start | bytes 1835008 | tf_op jit(solution)/shard_map/all_to_all | solution.py:51
Sparse Core Ops, SparseCore 0:
  52.0 89.0 all-reduce.2
where the time goes:
time: 177 us
  waiting for transfers between devices  102 us (58%)
  local copies, waits for them, and re-layouts  32.4 us (18%)
  matrix products  16.2 us (9%)
  between operations  13.6 us (8%)
  starting transfers between devices  7.71 us (4%)
  other arithmetic  5.03 us (3%)
    psum x1, waiting for transfers between devices, per_device(): summed = lax.psum(partial_rows, 'replica').astype(jnp.float32)  89.2 us
    unnamed x3, local copies, waits for them, and re-layouts  16.1 us
    all_to_all x1, waiting for transfers between devices, per_device(): lax.all_to_all(expert_rows, 'expert', split_axis=0, concat_axis=0, tiled=...  12.6 us
    dot_general x1, matrix products, per_device(): jnp.dot(slot_block.reshape(group_count * item_count, feature_count), pair...  10.3 us
    reshape x2, local copies, waits for them, and re-layouts, per_device(): partial_sum.astype(jnp.bfloat16)  6.97 us
    dot_general x1, matrix products, per_device(): jnp.dot(hidden.reshape(-1, hidden_width), down_local, preferred_element_t...  5.03 us
    all_to_all x1, starting transfers between devices, per_device(): lax.all_to_all(outgoing, 'expert', split_axis=0, concat_axis=0, tiled=True)  4.2 us
  transfers between devices with their start and end apart: 3, of which 2 were waited for; matrix products, arithmetic and copies ran while one was open for 9% of the time, Pallas kernels for 0%

commit v1 on v0

v1 whole, which is shorter than its diff:
```python
import functools

import jax
import jax.numpy as jnp
from jax import lax
from jax.experimental import pallas as pl
from jax.experimental.pallas import tpu as pltpu
from jax.sharding import PartitionSpec as P

MESH = pl.DeviceIdType.MESH
LANES = 128
SUBS = 2
LAG = 3


def slot_table(expert_ids, expert_count, stride):
    labels = lax.broadcasted_iota(jnp.int32, (1, 1, expert_count), 2)
    chosen = (expert_ids[:, :, None] == labels).astype(jnp.int32)
    per_row = jnp.sum(chosen, axis=1)
    before = jnp.cumsum(per_row, axis=0) - per_row
    slot_rank = jnp.sum(chosen * before[:, None, :], axis=2)
    return expert_ids * stride + slot_rank


def layer_kernel(
    n, depth, order, tokens, slots_t, slots, weights, gate_up, down, out,
    w_buf, d_buf, outgoing, x_buf, xs, acc, rs_in, rs_out, hid, res, ret,
    w_sem, d_sem, disp_s, disp_r, rs_s, rs_r, ag_s, ag_r, ret_s, ret_r,
):
    groups = lax.axis_index("groups")
    me = lax.axis_index("expert")
    z = lax.axis_index("replica")
    chip, core = me // 2, me % 2
    slot_rows = x_buf.shape[1]
    width = x_buf.shape[2]
    hidden = d_buf.shape[0]
    half = hidden // 2
    sub = half // SUBS
    blocks = sub // LANES
    units = n * SUBS
    sink = (0, depth - 1)
    source = (depth - 1, 0)
    onward = (z - 1, z + 1)
    back = (z + 1, z - 1)

    def w_copy(block):
        return pltpu.make_async_copy(
            gate_up.at[0, :, :, pl.ds(pl.multiple_of(block * LANES, LANES), LANES)],
            w_buf.at[block],
            w_sem.at[block],
        )

    for s in range(SUBS):
        for way in range(2):
            for i in range(blocks):
                w_copy((way * SUBS + s) * blocks + i).start()
    d_copy = pltpu.make_async_copy(down.at[0], d_buf, d_sem.at[0])
    d_copy.start()

    def partner(a, b, sign):
        return ((chip + sign * a + n // 2) % (n // 2)) * 2 + (core + b) % 2

    barrier = pltpu.get_barrier_semaphore()
    for a, b in order[1:]:
        pl.semaphore_signal(
            barrier, inc=1, device_id=(groups, partner(a, b, 1), z), device_id_type=MESH
        )

    @pl.when(z > 0)
    def _():
        pl.semaphore_signal(barrier, inc=1, device_id=(groups, me, z - 1), device_id_type=MESH)

    @pl.when(z < depth - 1)
    def _():
        pl.semaphore_signal(barrier, inc=1, device_id=(groups, me, z + 1), device_id_type=MESH)

    def pick(target):
        label = lax.broadcasted_iota(jnp.int32, (slot_rows, tokens.shape[0]), 0)
        label = label + target * slot_rows
        total = jnp.zeros(label.shape, jnp.float32)
        for k in range(slots_t.shape[0]):
            total = total + jnp.where(slots_t[k : k + 1, :] == label, 1.0, 0.0)
        return jnp.dot(
            total.astype(jnp.bfloat16), tokens[...], preferred_element_type=jnp.float32
        ).astype(jnp.bfloat16)

    x_buf[0] = pick(me)
    for k in range(1, n):
        a, b = order[k]
        outgoing[k - 1] = pick(partner(a, b, 1))

    at_end = jnp.logical_or(z == 0, z == depth - 1)

    @pl.when(at_end)
    def _():
        pl.semaphore_wait(barrier, n - 1 + min(1, depth - 1))

    @pl.when(jnp.logical_not(at_end))
    def _():
        pl.semaphore_wait(barrier, n + 1)

    def disp_copy(k, target):
        return pltpu.make_async_remote_copy(
            src_ref=outgoing.at[k - 1],
            dst_ref=x_buf.at[k],
            send_sem=disp_s.at[k],
            recv_sem=disp_r.at[k],
            device_id=(groups, target, z),
            device_id_type=MESH,
        )

    for k in range(1, n):
        a, b = order[k]
        disp_copy(k, partner(a, b, 1)).start()

    def rs_copy(u, way):
        return pltpu.make_async_remote_copy(
            src_ref=rs_out.at[u, way],
            dst_ref=rs_in.at[u, way],
            send_sem=rs_s.at[u, way],
            recv_sem=rs_r.at[u, way],
            device_id=(groups, me, onward[way]),
            device_id_type=MESH,
        )

    def ag_copy(u, way):
        return pltpu.make_async_remote_copy(
            src_ref=hid.at[u, way],
            dst_ref=hid.at[u, way],
            send_sem=ag_s.at[u, way],
            recv_sem=ag_r.at[u, way],
            device_id=(groups, me, back[way]),
            device_id_type=MESH,
        )

    def ret_copy(k, target):
        return pltpu.make_async_remote_copy(
            src_ref=res.at[k],
            dst_ref=ret.at[me],
            send_sem=ret_s.at[k],
            recv_sem=ret_r.at[k],
            device_id=(groups, target, z),
            device_id_type=MESH,
        )

    row = lax.broadcasted_iota(jnp.int32, (LANES, 2 * LANES), 0)
    column = lax.broadcasted_iota(jnp.int32, (LANES, 2 * LANES), 1)
    spread = [
        jnp.where(column == 2 * row + j, 1.0, 0.0).astype(jnp.bfloat16) for j in range(2)
    ]

    def reduce_step(u):
        k, s = u // SUBS, u % SUBS

        @pl.when(s == 0)
        def _():
            @pl.when(k > 0)
            def _():
                disp_copy(k, me).wait_recv()

            for block in range(width // LANES):
                part = x_buf[k, :, block * LANES : (block + 1) * LANES]
                for j in range(2):
                    xs[
                        j * slot_rows : (j + 1) * slot_rows,
                        2 * block * LANES : 2 * (block + 1) * LANES,
                    ] = jnp.dot(
                        part, spread[j], preferred_element_type=jnp.float32
                    ).astype(jnp.bfloat16)

        for way in range(2):
            first = (way * SUBS + s) * blocks

            @pl.when(u < SUBS)
            def _():
                for i in range(blocks):
                    w_copy(first + i).wait()

            for pair in range(blocks // 2):
                w = jnp.concatenate(
                    [
                        w_buf[first + 2 * pair + i].reshape(2 * width, LANES)
                        for i in range(2)
                    ],
                    axis=1,
                )
                acc[:, pair * 2 * LANES : (pair + 1) * 2 * LANES] = jnp.dot(
                    xs[...], w, preferred_element_type=jnp.float32
                )

            @pl.when(z != source[way])
            def _():
                rs_copy(u, way).wait_recv()
                acc[...] += rs_in[u, way].astype(jnp.float32)

            @pl.when(z != sink[way])
            def _():
                rs_out[u, way] = acc[...].astype(jnp.bfloat16)
                rs_copy(u, way).start()

            @pl.when(z == sink[way])
            def _():
                gate = acc[:slot_rows]
                hid[u, way] = (gate / (1.0 + jnp.exp(-gate)) * acc[slot_rows:]).astype(
                    jnp.bfloat16
                )
                ag_copy(u, way).start()

    def gather_step(v):
        k, s = v // SUBS, v % SUBS
        for way in range(2):

            @pl.when(z != sink[way])
            def _():
                ag_copy(v, way).wait_recv()

                @pl.when(z != source[way])
                def _():
                    ag_copy(v, way).start()

        @pl.when(s == SUBS - 1)
        def _():
            @pl.when(k == 0)
            def _():
                d_copy.wait()

            total = jnp.zeros((slot_rows, width), jnp.float32)
            for way in range(2):
                for i in range(SUBS):
                    start = way * half + i * sub
                    total = total + jnp.dot(
                        hid[k * SUBS + i, way],
                        d_buf[start : start + sub, :],
                        preferred_element_type=jnp.float32,
                    )

            @pl.when(k == 0)
            def _():
                ret[me] = total.astype(jnp.bfloat16)

            for kk in range(1, n):
                a, b = order[kk]

                @pl.when(k == kk)
                def _():
                    res[kk] = total.astype(jnp.bfloat16)
                    ret_copy(kk, partner(a, b, -1)).start()

    def step(u, carry):
        @pl.when(u < units)
        def _():
            reduce_step(u)

        @pl.when(u >= LAG)
        def _():
            gather_step(u - LAG)

        return carry

    lax.fori_loop(0, units + LAG, step, 0)

    def drain(u, carry):
        for way in range(2):

            @pl.when(z != sink[way])
            def _():
                rs_copy(u, way).wait_send()

            @pl.when(z != source[way])
            def _():
                ag_copy(u, way).wait_send()

        return carry

    lax.fori_loop(0, units, drain, 0)
    for k in range(1, n):
        disp_copy(k, me).wait_send()
        ret_copy(k, me).wait_send()
    for k in range(1, n):
        a, b = order[k]
        pltpu.make_async_remote_copy(
            src_ref=res.at[k],
            dst_ref=ret.at[partner(a, b, 1)],
            send_sem=ret_s.at[k],
            recv_sem=ret_r.at[k],
            device_id=(groups, me, z),
            device_id_type=MESH,
        ).wait_recv()

    rows = tokens.shape[0]
    label = lax.broadcasted_iota(jnp.int32, (rows, n * slot_rows), 1)
    chosen = [
        jnp.where(slots[:, k : k + 1] == label, 1.0, 0.0).astype(jnp.bfloat16)
        for k in range(slots.shape[1])
    ]
    tile = 2 * LANES if width % (2 * LANES) == 0 else LANES
    for c in range(width // tile):
        part = ret[:, :, c * tile : (c + 1) * tile].reshape(n * slot_rows, tile)
        mixed = jnp.zeros((rows, tile), jnp.float32)
        for k in range(slots.shape[1]):
            mixed = mixed + weights[:, k : k + 1] * jnp.dot(
                chosen[k], part, preferred_element_type=jnp.float32
            )
        out[:, c * tile : (c + 1) * tile] = mixed.astype(jnp.bfloat16)


def per_device(tokens, expert_ids, affinity, gate_up, down_proj):
    n = lax.axis_size("expert")
    depth = lax.axis_size("replica")
    rows, top = expert_ids.shape
    capacity = 5 * rows * top // (4 * n)
    slot_rows = -(-capacity // 16) * 16
    width = tokens.shape[1]
    hidden = down_proj.shape[1]
    slots = slot_table(expert_ids, n, slot_rows)
    weights = 2.5 * affinity / jnp.sum(affinity, axis=1, keepdims=True)
    order = [(0, 0)] + [(a, b) for a in range(1, n // 2) for b in range(2)] + [(0, 1)]
    units = n * SUBS
    sub = hidden // 2 // SUBS
    bf16 = jnp.bfloat16
    dma = pltpu.SemaphoreType.DMA
    vmem = pl.BlockSpec(memory_space=pltpu.VMEM)
    hbm = pl.BlockSpec(memory_space=pl.ANY)
    return pl.pallas_call(
        functools.partial(layer_kernel, n, depth, order),
        out_shape=jax.ShapeDtypeStruct((rows, width), bf16),
        in_specs=[vmem, vmem, vmem, vmem, hbm, hbm],
        out_specs=vmem,
        scratch_shapes=[
            pltpu.VMEM((hidden // LANES, width, 2, LANES), bf16),
            pltpu.VMEM((hidden, width), bf16),
            pltpu.VMEM((n - 1, slot_rows, width), bf16),
            pltpu.VMEM((n, slot_rows, width), bf16),
            pltpu.VMEM((2 * slot_rows, 2 * width), bf16),
            pltpu.VMEM((2 * slot_rows, sub), jnp.float32),
            pltpu.VMEM((units, 2, 2 * slot_rows, sub), bf16),
            pltpu.VMEM((units, 2, 2 * slot_rows, sub), bf16),
            pltpu.VMEM((units, 2, slot_rows, sub), bf16),
            pltpu.VMEM((n, slot_rows, width), bf16),
            pltpu.VMEM((n, slot_rows, width), bf16),
            dma((hidden // LANES,)),
            dma((1,)),
            dma((n,)),
            dma((n,)),
            dma((units, 2)),
            dma((units, 2)),
            dma((units, 2)),
            dma((units, 2)),
            dma((n,)),
            dma((n,)),
        ],
        compiler_params=pltpu.CompilerParams(
            collective_id=0, has_side_effects=True, vmem_limit_bytes=60 * 1024 * 1024
        ),
    )(tokens, slots.T, slots, weights, gate_up, down_proj)


def solution(mesh):
    placed = (
        P(("groups", "expert"), "replica"),
        P(("groups", "expert"), None),
        P(("groups", "expert"), None),
        P("expert", "replica", None, None),
        P("expert", None, "replica"),
    )
    return jax.shard_map(
        per_device,
        mesh=mesh,
        in_specs=placed,
        out_specs=P(("groups", "expert"), "replica"),
        check_vma=False,
    )
```

time: 177 us -> 277 us (1.56)
  Pallas kernels: 0 us -> 271 us
  waiting for transfers between devices: 102 us -> 0 us
  local copies, waits for them, and re-layouts: 32.4 us -> 2.74 us
  matrix products: 16.2 us -> 0 us
  between operations: 13.6 us -> 0.02 us
  starting transfers between devices: 7.71 us -> 0 us
    pallas_call x0 -> x1, Pallas kernels: none -> 271 us  [per_device(): pl.pallas_call(functools.partial(layer_kernel, n, depth, order), out_shap...]
    psum x1 -> x0, waiting for transfers between devices: 89.2 us -> none  [per_device(): summed = lax.psum(partial_rows, 'replica').astype(jnp.float32)]
    dot_general x3 -> x0, matrix products: 16.2 us -> none  [the longest x1 10.3 us: per_device(): jnp.dot(slot_block.reshape(group_count * item_count, feature_count), pair...]
    unnamed x3, local copies, waits for them, and re-layouts: 16.1 us -> 1.73 us
    all_to_all x2 -> x0, waiting for transfers between devices: 12.6 us -> none  [the longest x1 12.6 us: per_device(): lax.all_to_all(expert_rows, 'expert', split_axis=0, concat_axis=0, tiled=...]
    reshape x8 -> x0, local copies, waits for them, and re-layouts: 9.74 us -> none  [the longest x2 6.97 us: per_device(): partial_sum.astype(jnp.bfloat16)]
    all_to_all x2 -> x0, starting transfers between devices: 7.71 us -> none  [the longest x1 4.2 us: per_device(): lax.all_to_all(outgoing, 'expert', split_axis=0, concat_axis=0, tiled=True)]
  transfers between devices with their start and end apart: 3 -> 0, of which waited for: 2 -> 0; matrix products, arithmetic and copies ran while one was open for 9% -> 0% of each run, Pallas kernels for 0% -> 0%
where the time goes in v1:
time: 277 us
  Pallas kernels  271 us (98%)
  other arithmetic  3.62 us (1%)
    pallas_call x1, Pallas kernels, per_device(): pl.pallas_call(functools.partial(layer_kernel, n, depth, order), out_shap...  271 us

profile of v1, /device:TPU:0, one launch (start us, length us, event | category | flops | bytes accessed | tf_op | source)
XLA Modules:
  0.0 277.0 jit_solution(11587788835765450944)
XLA Ops:
  0.0 0.7 fusion
  0.7 0.7 convert_reduce_fusion
  1.4 0.1 copy.21
  1.5 0.1 reduce_window_sum.11
  1.6 0.1 copy.23
  1.7 0.7 select_reduce_fusion
  2.4 0.7 multiply_add_fusion
  3.1 0.0 copy-start
  3.1 0.7 copy.26.slots
  3.8 0.1 copy.24
  3.9 0.7 broadcast_divide_fusion.weights
  4.6 0.0 copy-done
  4.6 270.6 %shard_map.55 = bf16[96,1792]{1,0:T(8,128)(2,1)} custom-call(bf16[96,1792]{1,0:T(8,128)(2,1)} %tokens.1, s32[2,96]{1,0:T(2,128)} %bitcast.1, s32[96,2]{1,0:T(8,128)} %copy.26.slots, f32[96,2]{1,0:T(8,128)} %broadcast_divide_fusion.weights, bf16[1,1792,2,2048]{3,2,1,0:T(2,128)(2,1)} %gate_up.1, bf16[1,2048,1792]{2,1,0:T(8,128)(2,1)} %down.1), custom_call_target="tpu_custom_call" | custom-call | tf_op jit(solution)/shard_map/pallas_call | solution.py:324
  275.2 1.7 copy.28
  (1 shorter events, 0.0 us)
Async XLA Ops:
  3.1 1.5 copy-start

commit v2 on v1

--- a/solution.py
+++ b/solution.py
@@ -10,6 +10,7 @@
 MESH = pl.DeviceIdType.MESH
 LANES = 128
 SUBS = 2
+PIECES = 4
 LAG = 3
 
 
@@ -36,24 +37,27 @@
     hidden = d_buf.shape[0]
     half = hidden // 2
     sub = half // SUBS
-    blocks = sub // LANES
     units = n * SUBS
     sink = (0, depth - 1)
     source = (depth - 1, 0)
     onward = (z - 1, z + 1)
     back = (z + 1, z - 1)
 
-    def w_copy(block):
+    cut = 2 * width // PIECES
+
+    def w_copy(block, piece):
         return pltpu.make_async_copy(
-            gate_up.at[0, :, :, pl.ds(pl.multiple_of(block * LANES, LANES), LANES)],
-            w_buf.at[block],
-            w_sem.at[block],
+            gate_up.at[0]
+            .reshape(2 * width, hidden)
+            .at[pl.ds(piece * cut, cut), pl.ds(pl.multiple_of(block * sub, sub), sub)],
+            w_buf.at[block, pl.ds(piece * cut, cut)],
+            w_sem.at[block, piece],
         )
 
     for s in range(SUBS):
         for way in range(2):
-            for i in range(blocks):
-                w_copy((way * SUBS + s) * blocks + i).start()
+            for piece in range(PIECES):
+                w_copy(way * SUBS + s, piece).start()
     d_copy = pltpu.make_async_copy(down.at[0], d_buf, d_sem.at[0])
     d_copy.start()
 
@@ -169,24 +173,14 @@
                     ).astype(jnp.bfloat16)
 
         for way in range(2):
-            first = (way * SUBS + s) * blocks
+            block = way * SUBS + s
 
             @pl.when(u < SUBS)
             def _():
-                for i in range(blocks):
-                    w_copy(first + i).wait()
-
-            for pair in range(blocks // 2):
-                w = jnp.concatenate(
-                    [
-                        w_buf[first + 2 * pair + i].reshape(2 * width, LANES)
-                        for i in range(2)
-                    ],
-                    axis=1,
-                )
-                acc[:, pair * 2 * LANES : (pair + 1) * 2 * LANES] = jnp.dot(
-                    xs[...], w, preferred_element_type=jnp.float32
-                )
+                for piece in range(PIECES):
+                    w_copy(block, piece).wait()
+
+            acc[...] = jnp.dot(xs[...], w_buf[block], preferred_element_type=jnp.float32)
 
             @pl.when(z != source[way])
             def _():
@@ -327,7 +321,7 @@
         in_specs=[vmem, vmem, vmem, vmem, hbm, hbm],
         out_specs=vmem,
         scratch_shapes=[
-            pltpu.VMEM((hidden // LANES, width, 2, LANES), bf16),
+            pltpu.VMEM((2 * SUBS, 2 * width, sub), bf16),
             pltpu.VMEM((hidden, width), bf16),
             pltpu.VMEM((n - 1, slot_rows, width), bf16),
             pltpu.VMEM((n, slot_rows, width), bf16),
@@ -338,7 +332,7 @@
             pltpu.VMEM((units, 2, slot_rows, sub), bf16),
             pltpu.VMEM((n, slot_rows, width), bf16),
             pltpu.VMEM((n, slot_rows, width), bf16),
-            dma((hidden // LANES,)),
+            dma((2 * SUBS, PIECES)),
             dma((1,)),
             dma((n,)),
             dma((n,)),

time: 277 us -> 258 us (0.931)
  Pallas kernels: 271 us -> 251 us
    pallas_call x1, Pallas kernels: 271 us -> 251 us  [per_device(): pl.pallas_call(functools.partial(layer_kernel, n, depth, order), out_shap...]
where the time goes in v2:
time: 258 us
  Pallas kernels  251 us (97%)
  other arithmetic  3.62 us (1%)
  local copies, waits for them, and re-layouts  2.74 us (1%)
    pallas_call x1, Pallas kernels, per_device(): pl.pallas_call(functools.partial(layer_kernel, n, depth, order), out_shap...  251 us

profile of v2, /device:TPU:0, one launch (start us, length us, event | category | flops | bytes accessed | tf_op | source)
XLA Modules:
  0.0 257.5 jit_solution(5505992818669967768)
XLA Ops:
  0.0 0.7 fusion
  0.7 0.7 convert_reduce_fusion
  1.4 0.1 copy.21
  1.5 0.1 reduce_window_sum.11
  1.6 0.1 copy.23
  1.7 0.7 select_reduce_fusion
  2.4 0.7 multiply_add_fusion
  3.1 0.0 copy-start
  3.1 0.7 copy.26.slots
  3.8 0.1 copy.24
  3.9 0.7 broadcast_divide_fusion.weights
  4.6 0.0 copy-done
  4.6 251.1 %shard_map.55 = bf16[96,1792]{1,0:T(8,128)(2,1)} custom-call(bf16[96,1792]{1,0:T(8,128)(2,1)} %tokens.1, s32[2,96]{1,0:T(2,128)} %bitcast.1, s32[96,2]{1,0:T(8,128)} %copy.26.slots, f32[96,2]{1,0:T(8,128)} %broadcast_divide_fusion.weights, bf16[1,1792,2,2048]{3,2,1,0:T(2,128)(2,1)} %gate_up.1, bf16[1,2048,1792]{2,1,0:T(8,128)(2,1)} %down.1), custom_call_target="tpu_custom_call" | custom-call | tf_op jit(solution)/shard_map/pallas_call | solution.py:318
  255.8 1.7 copy.28
  (1 shorter events, 0.0 us)
Async XLA Ops:
  3.1 1.5 copy-start

commit v3 on v2

--- a/solution.py
+++ b/solution.py
@@ -9,9 +9,9 @@
 
 MESH = pl.DeviceIdType.MESH
 LANES = 128
-SUBS = 2
-PIECES = 4
-LAG = 3
+SUBS = 4
+PIECES = 2
+SKEW = 2
 
 
 def slot_table(expert_ids, expert_count, stride):
@@ -153,105 +153,134 @@
         jnp.where(column == 2 * row + j, 1.0, 0.0).astype(jnp.bfloat16) for j in range(2)
     ]
 
-    def reduce_step(u):
-        k, s = u // SUBS, u % SUBS
-
-        @pl.when(s == 0)
-        def _():
-            @pl.when(k > 0)
-            def _():
-                disp_copy(k, me).wait_recv()
-
-            for block in range(width // LANES):
-                part = x_buf[k, :, block * LANES : (block + 1) * LANES]
-                for j in range(2):
-                    xs[
-                        j * slot_rows : (j + 1) * slot_rows,
-                        2 * block * LANES : 2 * (block + 1) * LANES,
-                    ] = jnp.dot(
-                        part, spread[j], preferred_element_type=jnp.float32
-                    ).astype(jnp.bfloat16)
-
-        for way in range(2):
-            block = way * SUBS + s
-
-            @pl.when(u < SUBS)
-            def _():
-                for piece in range(PIECES):
-                    w_copy(block, piece).wait()
-
-            acc[...] = jnp.dot(xs[...], w_buf[block], preferred_element_type=jnp.float32)
-
-            @pl.when(z != source[way])
-            def _():
-                rs_copy(u, way).wait_recv()
-                acc[...] += rs_in[u, way].astype(jnp.float32)
-
-            @pl.when(z != sink[way])
-            def _():
-                rs_out[u, way] = acc[...].astype(jnp.bfloat16)
-                rs_copy(u, way).start()
-
-            @pl.when(z == sink[way])
-            def _():
-                gate = acc[:slot_rows]
-                hid[u, way] = (gate / (1.0 + jnp.exp(-gate)) * acc[slot_rows:]).astype(
+    position = (depth - 1 - z, z)
+    nearest = jnp.minimum(position[0], position[1])
+    furthest = jnp.maximum(position[0], position[1])
+    fill = SKEW * (depth - 1)
+
+    def live(u):
+        return jnp.logical_and(u >= 0, u < units)
+
+    def widen(k):
+        @pl.when(k > 0)
+        def _():
+            disp_copy(k, me).wait_recv()
+
+        for block in range(width // LANES):
+            part = x_buf[k, :, block * LANES : (block + 1) * LANES]
+            for j in range(2):
+                xs[
+                    k,
+                    j * slot_rows : (j + 1) * slot_rows,
+                    2 * block * LANES : 2 * (block + 1) * LANES,
+                ] = jnp.dot(part, spread[j], preferred_element_type=jnp.float32).astype(
                     jnp.bfloat16
                 )
-                ag_copy(u, way).start()
-
-    def gather_step(v):
-        k, s = v // SUBS, v % SUBS
-        for way in range(2):
-
-            @pl.when(z != sink[way])
-            def _():
-                ag_copy(v, way).wait_recv()
-
-                @pl.when(z != source[way])
-                def _():
-                    ag_copy(v, way).start()
-
-        @pl.when(s == SUBS - 1)
-        def _():
-            @pl.when(k == 0)
-            def _():
-                d_copy.wait()
-
-            total = jnp.zeros((slot_rows, width), jnp.float32)
-            for way in range(2):
-                for i in range(SUBS):
-                    start = way * half + i * sub
-                    total = total + jnp.dot(
-                        hid[k * SUBS + i, way],
-                        d_buf[start : start + sub, :],
-                        preferred_element_type=jnp.float32,
-                    )
-
-            @pl.when(k == 0)
-            def _():
-                ret[me] = total.astype(jnp.bfloat16)
-
-            for kk in range(1, n):
-                a, b = order[kk]
-
-                @pl.when(k == kk)
-                def _():
-                    res[kk] = total.astype(jnp.bfloat16)
-                    ret_copy(kk, partner(a, b, -1)).start()
-
-    def step(u, carry):
-        @pl.when(u < units)
-        def _():
-            reduce_step(u)
-
-        @pl.when(u >= LAG)
-        def _():
-            gather_step(u - LAG)
+
+    def multiply(u, way):
+        block = way * SUBS + u % SUBS
+
+        @pl.when(u < SUBS)
+        def _():
+            for piece in range(PIECES):
+                w_copy(block, piece).wait()
+
+        acc[way] = jnp.dot(
+            xs[u // SUBS], w_buf[block], preferred_element_type=jnp.float32
+        )
+
+    def reduce_step(u, way):
+        @pl.when(z != source[way])
+        def _():
+            rs_copy(u, way).wait_recv()
+            acc[way] += rs_in[u, way].astype(jnp.float32)
+
+        @pl.when(z != sink[way])
+        def _():
+            rs_out[u, way] = acc[way].astype(jnp.bfloat16)
+            rs_copy(u, way).start()
+
+        @pl.when(z == sink[way])
+        def _():
+            gate = acc[way, :slot_rows]
+            hid[u, way] = (gate / (1.0 + jnp.exp(-gate)) * acc[way, slot_rows:]).astype(
+                jnp.bfloat16
+            )
+            ag_copy(u, way).start()
+
+    def gather_step(v, way):
+        @pl.when(z != sink[way])
+        def _():
+            ag_copy(v, way).wait_recv()
+
+            @pl.when(z != source[way])
+            def _():
+                ag_copy(v, way).start()
+
+    def project(k):
+        @pl.when(k == 0)
+        def _():
+            d_copy.wait()
+
+        total = jnp.zeros((slot_rows, width), jnp.float32)
+        for way in range(2):
+            for i in range(SUBS):
+                start = way * half + i * sub
+                total = total + jnp.dot(
+                    hid[k * SUBS + i, way],
+                    d_buf[start : start + sub, :],
+                    preferred_element_type=jnp.float32,
+                )
+
+        @pl.when(k == 0)
+        def _():
+            ret[me] = total.astype(jnp.bfloat16)
+
+        for kk in range(1, n):
+            a, b = order[kk]
+
+            @pl.when(k == kk)
+            def _():
+                res[kk] = total.astype(jnp.bfloat16)
+                ret_copy(kk, partner(a, b, -1)).start()
+
+    def step(t, carry):
+        lead = t - SKEW * nearest
+
+        @pl.when(jnp.logical_and(live(lead), lead % SUBS == 0))
+        def _():
+            widen(lead // SUBS)
+
+        for way in range(2):
+            u = t - SKEW * position[way]
+
+            @pl.when(live(u))
+            def _():
+                multiply(u, way)
+
+        for way in range(2):
+            u = t - SKEW * position[way]
+
+            @pl.when(live(u))
+            def _():
+                reduce_step(u, way)
+
+        for way in range(2):
+            v = t - fill - SKEW * (depth - 1 - position[way])
+
+            @pl.when(live(v))
+            def _():
+                gather_step(v, way)
+
+        trail = t - fill - SKEW * furthest
+
+        @pl.when(jnp.logical_and(live(trail), trail % SUBS == SUBS - 1))
+        def _():
+            project(trail // SUBS)
 
         return carry
 
-    lax.fori_loop(0, units + LAG, step, 0)
+    lax.fori_loop(0, units + 2 * fill, step, 0)
 
     def drain(u, carry):
         for way in range(2):
@@ -325,8 +354,8 @@
             pltpu.VMEM((hidden, width), bf16),
             pltpu.VMEM((n - 1, slot_rows, width), bf16),
             pltpu.VMEM((n, slot_rows, width), bf16),
-            pltpu.VMEM((2 * slot_rows, 2 * width), bf16),
-            pltpu.VMEM((2 * slot_rows, sub), jnp.float32),
+            pltpu.VMEM((n, 2 * slot_rows, 2 * width), bf16),
+            pltpu.VMEM((2, 2 * slot_rows, sub), jnp.float32),
             pltpu.VMEM((units, 2, 2 * slot_rows, sub), bf16),
             pltpu.VMEM((units, 2, 2 * slot_rows, sub), bf16),
             pltpu.VMEM((units, 2, slot_rows, sub), bf16),

time: 258 us -> 69.1 us (0.27)
  Pallas kernels: 251 us -> 62.5 us
    pallas_call x1, Pallas kernels: 251 us -> 62.5 us  [per_device(): pl.pallas_call(functools.partial(layer_kernel, n, depth, order), out_shap...]
where the time goes in v3:
time: 69.1 us; the launch traced here: 68.9 us
  Pallas kernels  62.5 us (90%)
  other arithmetic  3.62 us (5%)
  local copies, waits for them, and re-layouts  2.74 us (4%)
    pallas_call x1, Pallas kernels, per_device(): pl.pallas_call(functools.partial(layer_kernel, n, depth, order), out_shap...  62.5 us
    unnamed x3, local copies, waits for them, and re-layouts  1.73 us

profile of v3, /device:TPU:0, one launch (start us, length us, event | category | flops | bytes accessed | tf_op | source)
XLA Modules:
  0.0 68.9 jit_solution(18197747499992990923)
XLA Ops:
  0.0 0.7 %fusion = (f32[96]{0:T(128)S(1)}, f32[96,2]{0,1:T(2,128)S(1)}) fusion(f32[96,2]{0,1:T(2,128)} %param.7), kind=kLoop, calls=%fused_computation.6 | loop fusion | flops 288 | bytes 1920 | tf_op jit(solution)/shard_map/reduce_sum | solution.py:339
  0.7 0.7 %convert_reduce_fusion = s32[96,4]{0,1:T(4,128)S(1)} fusion(s32[96,2]{0,1:T(2,128)} %param.6), kind=kLoop, calls=%fused_computation.2 | loop fusion | flops 1920 | bytes 2304 | tf_op jit(solution)/shard_map/reduce_sum | solution.py:20
  1.4 0.1 copy.21
  1.5 0.1 reduce_window_sum.11
  1.6 0.1 copy.23
  1.7 0.7 %select_reduce_fusion = s32[96,2]{0,1:T(2,128)S(1)} fusion(s32[96,4]{0,1:T(4,128)S(1)} %copy.23, s32[96,2]{0,1:T(2,128)} %param.6), kind=kLoop, calls=%fused_computation.1 | loop fusion | flops 2112 | bytes 3072 | tf_op jit(solution)/shard_map/reduce_sum | solution.py:22
  2.4 0.7 multiply_add_fusion
  3.1 0.0 copy-start
  3.1 0.7 %copy.26.slots = s32[96,2]{1,0:T(8,128)} copy(s32[96,2]{0,1:T(2,128)S(1)} %multiply_add_fusion) | data formatting | bytes 1536 | tf_op jit(solution)/shard_map/add | solution.py:23
  3.8 0.1 copy.24
  3.9 0.7 %broadcast_divide_fusion.weights = f32[96,2]{1,0:T(8,128)} fusion(f32[96,2]{1,0:T(8,128)S(1)} %copy.24, f32[96]{0:T(128)S(1)} %get-tuple-element.5), kind=kLoop, calls=%fused_computation | loop fusion | flops 192 | bytes 1920 | tf_op jit(solution)/shard_map/div | solution.py:339
  4.6 0.0 copy-done
  4.6 62.5 %shard_map.55 = bf16[96,1792]{1,0:T(8,128)(2,1)} custom-call(bf16[96,1792]{1,0:T(8,128)(2,1)} %tokens.1, s32[2,96]{1,0:T(2,128)} %bitcast.1, s32[96,2]{1,0:T(8,128)} %copy.26.slots, f32[96,2]{1,0:T(8,128)} %broadcast_divide_fusion.weights, bf16[1,1792,2,2048]{3,2,1,0:T(2,128)(2,1)} %gate_up.1, bf16[1,2048,1792]{2,1,0:T(8,128)(2,1)} %down.1), custom_call_target="tpu_custom_call" | custom-call | tf_op jit(solution)/shard_map/pallas_call | solution.py:347
  67.2 1.7 %copy.28 = bf16[96,1792]{1,0:T(8,128)(2,1)} copy(bf16[96,1792]{1,0:T(8,128)(2,1)} %shard_map.55) | data formatting | bytes 688128
  (1 shorter events, 0.0 us)
Async XLA Ops:
  3.1 1.5 %copy-start = (s32[96,2]{0,1:T(2,128)}, s32[96,2]{0,1:T(2,128)S(1)}, u32[]{:S(2)}) copy-start(s32[96,2]{0,1:T(2,128)S(1)} %multiply_add_fusion) | copy-start | bytes 2308

commit v4 on v3

--- a/solution.py
+++ b/solution.py
@@ -11,21 +11,12 @@
 LANES = 128
 SUBS = 4
 PIECES = 2
-SKEW = 2
-
-
-def slot_table(expert_ids, expert_count, stride):
-    labels = lax.broadcasted_iota(jnp.int32, (1, 1, expert_count), 2)
-    chosen = (expert_ids[:, :, None] == labels).astype(jnp.int32)
-    per_row = jnp.sum(chosen, axis=1)
-    before = jnp.cumsum(per_row, axis=0) - per_row
-    slot_rank = jnp.sum(chosen * before[:, None, :], axis=2)
-    return expert_ids * stride + slot_rank
+SKEW = 3
 
 
 def layer_kernel(
-    n, depth, order, tokens, slots_t, slots, weights, gate_up, down, out,
-    w_buf, d_buf, outgoing, x_buf, xs, acc, rs_in, rs_out, hid, res, ret,
+    n, depth, order, tokens, ids_t, affinity_t, gate_up, down, out,
+    w_buf, d_buf, outgoing, x_buf, xs, acc, rs_in, rs_out, hid, res, ret, chosen, share,
     w_sem, d_sem, disp_s, disp_r, rs_s, rs_r, ag_s, ag_r, ret_s, ret_r,
 ):
     groups = lax.axis_index("groups")
@@ -54,10 +45,11 @@
             w_sem.at[block, piece],
         )
 
-    for s in range(SUBS):
-        for way in range(2):
+    left = 1 - (2 * z) // depth
+    for way in range(2):
+        for s in range(SUBS):
             for piece in range(PIECES):
-                w_copy(way * SUBS + s, piece).start()
+                w_copy(((way + left) % 2) * SUBS + s, piece).start()
     d_copy = pltpu.make_async_copy(down.at[0], d_buf, d_sem.at[0])
     d_copy.start()
 
@@ -78,14 +70,28 @@
     def _():
         pl.semaphore_signal(barrier, inc=1, device_id=(groups, me, z + 1), device_id_type=MESH)
 
+    rows = tokens.shape[0]
+    top = ids_t.shape[0]
+    f32 = jnp.float32
+    expert_label = lax.broadcasted_iota(jnp.int32, (-(-n // 16) * 16, rows), 0)
+    named = [ids_t[k : k + 1, :] == expert_label for k in range(top)]
+    per_row = sum(jnp.where(hit, 1.0, 0.0) for hit in named)
+    first = lax.broadcasted_iota(jnp.int32, (rows, rows), 0)
+    second = lax.broadcasted_iota(jnp.int32, (rows, rows), 1)
+    earlier = jnp.where(first < second, 1.0, 0.0).astype(jnp.bfloat16)
+    before = jnp.dot(per_row.astype(jnp.bfloat16), earlier, preferred_element_type=f32)
+    slot = [
+        ids_t[k : k + 1, :].astype(f32) * float(slot_rows)
+        + jnp.sum(jnp.where(named[k], before, 0.0), axis=0, keepdims=True)
+        for k in range(top)
+    ]
+
     def pick(target):
-        label = lax.broadcasted_iota(jnp.int32, (slot_rows, tokens.shape[0]), 0)
-        label = label + target * slot_rows
-        total = jnp.zeros(label.shape, jnp.float32)
-        for k in range(slots_t.shape[0]):
-            total = total + jnp.where(slots_t[k : k + 1, :] == label, 1.0, 0.0)
+        label = lax.broadcasted_iota(jnp.int32, (slot_rows, rows), 0)
+        label = (label + target * slot_rows).astype(f32)
+        total = sum(jnp.where(slot[k] == label, 1.0, 0.0) for k in range(top))
         return jnp.dot(
-            total.astype(jnp.bfloat16), tokens[...], preferred_element_type=jnp.float32
+            total.astype(jnp.bfloat16), tokens[...], preferred_element_type=f32
         ).astype(jnp.bfloat16)
 
     x_buf[0] = pick(me)
@@ -116,6 +122,17 @@
     for k in range(1, n):
         a, b = order[k]
         disp_copy(k, partner(a, b, 1)).start()
+
+    def column_of(line):
+        return jnp.sum(jnp.where(first == second, line, 0.0), axis=1, keepdims=True)
+
+    slot_label = lax.broadcasted_iota(jnp.int32, (rows, n * slot_rows), 1).astype(f32)
+    whole = sum(affinity_t[k : k + 1, :] for k in range(top))
+    for k in range(top):
+        chosen[k] = jnp.where(column_of(slot[k]) == slot_label, 1.0, 0.0).astype(jnp.bfloat16)
+        share[k] = jnp.broadcast_to(
+            column_of(2.5 * affinity_t[k : k + 1, :] / whole), share.shape[1:]
+        )
 
     def rs_copy(u, way):
         return pltpu.make_async_remote_copy(
@@ -310,18 +327,12 @@
             device_id_type=MESH,
         ).wait_recv()
 
-    rows = tokens.shape[0]
-    label = lax.broadcasted_iota(jnp.int32, (rows, n * slot_rows), 1)
-    chosen = [
-        jnp.where(slots[:, k : k + 1] == label, 1.0, 0.0).astype(jnp.bfloat16)
-        for k in range(slots.shape[1])
-    ]
     tile = 2 * LANES if width % (2 * LANES) == 0 else LANES
     for c in range(width // tile):
         part = ret[:, :, c * tile : (c + 1) * tile].reshape(n * slot_rows, tile)
         mixed = jnp.zeros((rows, tile), jnp.float32)
-        for k in range(slots.shape[1]):
-            mixed = mixed + weights[:, k : k + 1] * jnp.dot(
+        for k in range(top):
+            mixed = mixed + share[k, :, :1] * jnp.dot(
                 chosen[k], part, preferred_element_type=jnp.float32
             )
         out[:, c * tile : (c + 1) * tile] = mixed.astype(jnp.bfloat16)
@@ -335,8 +346,6 @@
     slot_rows = -(-capacity // 16) * 16
     width = tokens.shape[1]
     hidden = down_proj.shape[1]
-    slots = slot_table(expert_ids, n, slot_rows)
-    weights = 2.5 * affinity / jnp.sum(affinity, axis=1, keepdims=True)
     order = [(0, 0)] + [(a, b) for a in range(1, n // 2) for b in range(2)] + [(0, 1)]
     units = n * SUBS
     sub = hidden // 2 // SUBS
@@ -347,7 +356,7 @@
     return pl.pallas_call(
         functools.partial(layer_kernel, n, depth, order),
         out_shape=jax.ShapeDtypeStruct((rows, width), bf16),
-        in_specs=[vmem, vmem, vmem, vmem, hbm, hbm],
+        in_specs=[vmem, vmem, vmem, hbm, hbm],
         out_specs=vmem,
         scratch_shapes=[
             pltpu.VMEM((2 * SUBS, 2 * width, sub), bf16),
@@ -361,6 +370,8 @@
             pltpu.VMEM((units, 2, slot_rows, sub), bf16),
             pltpu.VMEM((n, slot_rows, width), bf16),
             pltpu.VMEM((n, slot_rows, width), bf16),
+            pltpu.VMEM((top, rows, n * slot_rows), bf16),
+            pltpu.VMEM((top, rows, LANES), jnp.float32),
             dma((2 * SUBS, PIECES)),
             dma((1,)),
             dma((n,)),
@@ -375,7 +386,7 @@
         compiler_params=pltpu.CompilerParams(
             collective_id=0, has_side_effects=True, vmem_limit_bytes=60 * 1024 * 1024
         ),
-    )(tokens, slots.T, slots, weights, gate_up, down_proj)
+    )(tokens, expert_ids.T, affinity.T, gate_up, down_proj)
 
 
 def solution(mesh):

time: 69.1 us -> 62.1 us (0.90)
  other arithmetic: 3.62 us -> 0 us
  Pallas kernels: 62.5 us -> 60.1 us
  local copies, waits for them, and re-layouts: 2.74 us -> 1.73 us
    pallas_call x1, Pallas kernels: 62.5 us -> 60.1 us  [per_device(): pl.pallas_call(functools.partial(layer_kernel, n, depth, order), out_shap...]
    reduce_sum x3 -> x0, other arithmetic: 2.1 us -> none  [the longest x1 0.71 us: slot_table(): slot_rank = jnp.sum(chosen * before[:, None, :], axis=2)]
    add x1 -> x0, local copies, waits for them, and re-layouts: 0.72 us -> none  [slot_table(): return expert_ids * stride + slot_rank]
    div x1 -> x0, other arithmetic: 0.7 us -> none  [per_device(): weights = 2.5 * affinity / jnp.sum(affinity, axis=1, keepdims=True)]
    unnamed x3 -> x1, local copies, waits for them, and re-layouts: 1.73 us -> 1.73 us
where the time goes in v4:
time: 62.1 us; the launch traced here: 61.9 us
  Pallas kernels  60.1 us (97%)
  local copies, waits for them, and re-layouts  1.73 us (3%)
    pallas_call x1, Pallas kernels, per_device(): pl.pallas_call(functools.partial(layer_kernel, n, depth, order), out_shap...  60.1 us
    unnamed x1, local copies, waits for them, and re-layouts  1.73 us

profile of v4, /device:TPU:0, one launch (start us, length us, event | category | flops | bytes accessed | tf_op | source)
XLA Modules:
  0.0 61.9 jit_solution(4893772152016604325)
XLA Ops:
  0.0 60.1 %shard_map.55 = bf16[96,1792]{1,0:T(8,128)(2,1)} custom-call(bf16[96,1792]{1,0:T(8,128)(2,1)} %tokens.1, s32[2,96]{1,0:T(2,128)} %bitcast.2, f32[2,96]{1,0:T(2,128)} %bitcast.3, bf16[1,1792,2,2048]{3,2,1,0:T(2,128)(2,1)} %gate_up.1, bf16[1,2048,1792]{2,1,0:T(8,128)(2,1)} %down.1), custom_call_target="tpu_custom_call" | custom-call | tf_op jit(solution)/shard_map/pallas_call | solution.py:356
  60.2 1.7 %copy.7 = bf16[96,1792]{1,0:T(8,128)(2,1)} copy(bf16[96,1792]{1,0:T(8,128)(2,1)} %shard_map.55) | data formatting | bytes 688128

commit v5 on v4

--- a/solution.py
+++ b/solution.py
@@ -16,7 +16,7 @@
 
 def layer_kernel(
     n, depth, order, tokens, ids_t, affinity_t, gate_up, down, out,
-    w_buf, d_buf, outgoing, x_buf, xs, acc, rs_in, rs_out, hid, res, ret, chosen, share,
+    w_buf, d_buf, outgoing, x_buf, xs, acc, rs_in, rs_out, hid, res, ret, chosen, share, total,
     w_sem, d_sem, disp_s, disp_r, rs_s, rs_r, ag_s, ag_r, ret_s, ret_r,
 ):
     groups = lax.axis_index("groups")
@@ -89,9 +89,9 @@
     def pick(target):
         label = lax.broadcasted_iota(jnp.int32, (slot_rows, rows), 0)
         label = (label + target * slot_rows).astype(f32)
-        total = sum(jnp.where(slot[k] == label, 1.0, 0.0) for k in range(top))
+        hits = sum(jnp.where(slot[k] == label, 1.0, 0.0) for k in range(top))
         return jnp.dot(
-            total.astype(jnp.bfloat16), tokens[...], preferred_element_type=f32
+            hits.astype(jnp.bfloat16), tokens[...], preferred_element_type=f32
         ).astype(jnp.bfloat16)
 
     x_buf[0] = pick(me)
@@ -234,31 +234,24 @@
             def _():
                 ag_copy(v, way).start()
 
-    def project(k):
+    def project(v, way):
+        k, s = v // SUBS, v % SUBS
+        start = pl.multiple_of((way * SUBS + s) * sub, sub)
+        total[k] += jnp.dot(
+            hid[v, way], d_buf[pl.ds(start, sub), :], preferred_element_type=f32
+        )
+
+    def send_back(k):
         @pl.when(k == 0)
         def _():
-            d_copy.wait()
-
-        total = jnp.zeros((slot_rows, width), jnp.float32)
-        for way in range(2):
-            for i in range(SUBS):
-                start = way * half + i * sub
-                total = total + jnp.dot(
-                    hid[k * SUBS + i, way],
-                    d_buf[start : start + sub, :],
-                    preferred_element_type=jnp.float32,
-                )
-
-        @pl.when(k == 0)
-        def _():
-            ret[me] = total.astype(jnp.bfloat16)
+            ret[me] = total[0].astype(jnp.bfloat16)
 
         for kk in range(1, n):
             a, b = order[kk]
 
             @pl.when(k == kk)
             def _():
-                res[kk] = total.astype(jnp.bfloat16)
+                res[kk] = total[kk].astype(jnp.bfloat16)
                 ret_copy(kk, partner(a, b, -1)).start()
 
     def step(t, carry):
@@ -289,11 +282,23 @@
             def _():
                 gather_step(v, way)
 
+        @pl.when(t == fill)
+        def _():
+            d_copy.wait()
+            total[...] = jnp.zeros_like(total)
+
+        for way in range(2):
+            v = t - fill - SKEW * (depth - 1 - position[way])
+
+            @pl.when(live(v))
+            def _():
+                project(v, way)
+
         trail = t - fill - SKEW * furthest
 
         @pl.when(jnp.logical_and(live(trail), trail % SUBS == SUBS - 1))
         def _():
-            project(trail // SUBS)
+            send_back(trail // SUBS)
 
         return carry
 
@@ -372,6 +377,7 @@
             pltpu.VMEM((n, slot_rows, width), bf16),
             pltpu.VMEM((top, rows, n * slot_rows), bf16),
             pltpu.VMEM((top, rows, LANES), jnp.float32),
+            pltpu.VMEM((n, slot_rows, width), jnp.float32),
             dma((2 * SUBS, PIECES)),
             dma((1,)),
             dma((n,)),

time: 62.1 us -> 60.6 us (0.976)
  Pallas kernels: 60.1 us -> 58.5 us
    pallas_call x1, Pallas kernels: 60.1 us -> 58.5 us  [per_device(): pl.pallas_call(functools.partial(layer_kernel, n, depth, order), out_shap...]
where the time goes in v5:
time: 60.6 us; the launch traced here: 60.3 us
  Pallas kernels  58.5 us (97%)
  local copies, waits for them, and re-layouts  1.73 us (3%)
    pallas_call x1, Pallas kernels, per_device(): pl.pallas_call(functools.partial(layer_kernel, n, depth, order), out_shap...  58.5 us
    unnamed x1, local copies, waits for them, and re-layouts  1.73 us

profile of v5, /device:TPU:0, one launch (start us, length us, event | category | flops | bytes accessed | tf_op | source)
XLA Modules:
  0.0 60.3 jit_solution(9157039303745443816)
XLA Ops:
  0.0 58.5 %shard_map.55 = bf16[96,1792]{1,0:T(8,128)(2,1)} custom-call(bf16[96,1792]{1,0:T(8,128)(2,1)} %tokens.1, s32[2,96]{1,0:T(2,128)} %bitcast.2, f32[2,96]{1,0:T(2,128)} %bitcast.3, bf16[1,1792,2,2048]{3,2,1,0:T(2,128)(2,1)} %gate_up.1, bf16[1,2048,1792]{2,1,0:T(8,128)(2,1)} %down.1), custom_call_target="tpu_custom_call" | custom-call | tf_op jit(solution)/shard_map/pallas_call | solution.py:361
  58.5 1.7 %copy.7 = bf16[96,1792]{1,0:T(8,128)(2,1)} copy(bf16[96,1792]{1,0:T(8,128)(2,1)} %shard_map.55) | data formatting | bytes 688128

commit v6 on v5

--- a/solution.py
+++ b/solution.py
@@ -16,7 +16,7 @@
 
 def layer_kernel(
     n, depth, order, tokens, ids_t, affinity_t, gate_up, down, out,
-    w_buf, d_buf, outgoing, x_buf, xs, acc, rs_in, rs_out, hid, res, ret, chosen, share, total,
+    w_buf, d_buf, outgoing, x_buf, xs, acc, rs_in, rs_out, hid, res, ret, chosen, share, total, stash,
     w_sem, d_sem, disp_s, disp_r, rs_s, rs_r, ag_s, ag_r, ret_s, ret_r,
 ):
     groups = lax.axis_index("groups")
@@ -202,9 +202,26 @@
             for piece in range(PIECES):
                 w_copy(block, piece).wait()
 
-        acc[way] = jnp.dot(
-            xs[u // SUBS], w_buf[block], preferred_element_type=jnp.float32
-        )
+        k, s = u // SUBS, u % SUBS
+        paired = k >= 2
+
+        @pl.when(k < 2)
+        def _():
+            acc[way] = jnp.dot(xs[k], w_buf[block], preferred_element_type=f32)
+
+        @pl.when(jnp.logical_and(paired, k % 2 == 0))
+        def _():
+            both = jnp.dot(
+                xs[pl.ds(k, 2)].reshape(4 * slot_rows, 2 * width),
+                w_buf[block],
+                preferred_element_type=f32,
+            )
+            acc[way] = both[: 2 * slot_rows]
+            stash[way, s] = both[2 * slot_rows :]
+
+        @pl.when(jnp.logical_and(paired, k % 2 == 1))
+        def _():
+            acc[way] = stash[way, s]
 
     def reduce_step(u, way):
         @pl.when(z != source[way])
@@ -259,7 +276,15 @@
 
         @pl.when(jnp.logical_and(live(lead), lead % SUBS == 0))
         def _():
-            widen(lead // SUBS)
+            k = lead // SUBS
+
+            @pl.when(jnp.logical_or(k < 2, k % 2 == 0))
+            def _():
+                widen(k)
+
+            @pl.when(jnp.logical_and(k >= 2, k % 2 == 0))
+            def _():
+                widen(k + 1)
 
         for way in range(2):
             u = t - SKEW * position[way]
@@ -378,6 +403,7 @@
             pltpu.VMEM((top, rows, n * slot_rows), bf16),
             pltpu.VMEM((top, rows, LANES), jnp.float32),
             pltpu.VMEM((n, slot_rows, width), jnp.float32),
+            pltpu.VMEM((2, SUBS, 2 * slot_rows, sub), jnp.float32),
             dma((2 * SUBS, PIECES)),
             dma((1,)),
             dma((n,)),

time: 60.6 us -> 61.4 us (1.013)
  no operation moved by 1% of the time
where the time goes in v6:
time: 61.4 us; the launch traced here: 60.8 us
  Pallas kernels  59 us (96%)
  local copies, waits for them, and re-layouts  1.73 us (3%)
    pallas_call x1, Pallas kernels, per_device(): pl.pallas_call(functools.partial(layer_kernel, n, depth, order), out_shap...  59 us
    unnamed x1, local copies, waits for them, and re-layouts  1.73 us

profile of v6, /device:TPU:0, one launch (start us, length us, event | category | flops | bytes accessed | tf_op | source)
XLA Modules:
  0.0 60.8 jit_solution(12436418339226285586)
XLA Ops:
  0.0 59.0 %shard_map.55 = bf16[96,1792]{1,0:T(8,128)(2,1)} custom-call(bf16[96,1792]{1,0:T(8,128)(2,1)} %tokens.1, s32[2,96]{1,0:T(2,128)} %bitcast.2, f32[2,96]{1,0:T(2,128)} %bitcast.3, bf16[1,1792,2,2048]{3,2,1,0:T(2,128)(2,1)} %gate_up.1, bf16[1,2048,1792]{2,1,0:T(8,128)(2,1)} %down.1), custom_call_target="tpu_custom_call" | custom-call | tf_op jit(solution)/shard_map/pallas_call | solution.py:386
  59.0 1.7 %copy.7 = bf16[96,1792]{1,0:T(8,128)(2,1)} copy(bf16[96,1792]{1,0:T(8,128)(2,1)} %shard_map.55) | data formatting | bytes 688128

commit v7 on v5

--- a/solution.py
+++ b/solution.py
@@ -128,11 +128,12 @@
 
     slot_label = lax.broadcasted_iota(jnp.int32, (rows, n * slot_rows), 1).astype(f32)
     whole = sum(affinity_t[k : k + 1, :] for k in range(top))
-    for k in range(top):
-        chosen[k] = jnp.where(column_of(slot[k]) == slot_label, 1.0, 0.0).astype(jnp.bfloat16)
-        share[k] = jnp.broadcast_to(
-            column_of(2.5 * affinity_t[k : k + 1, :] / whole), share.shape[1:]
-        )
+    def prepare_mix():
+        for k in range(top):
+            chosen[k] = jnp.where(column_of(slot[k]) == slot_label, 1.0, 0.0).astype(jnp.bfloat16)
+            share[k] = jnp.broadcast_to(
+                column_of(2.5 * affinity_t[k : k + 1, :] / whole), share.shape[1:]
+            )
 
     def rs_copy(u, way):
         return pltpu.make_async_remote_copy(
@@ -286,6 +287,7 @@
         def _():
             d_copy.wait()
             total[...] = jnp.zeros_like(total)
+            prepare_mix()
 
         for way in range(2):
             v = t - fill - SKEW * (depth - 1 - position[way])
@@ -340,7 +342,7 @@
             mixed = mixed + share[k, :, :1] * jnp.dot(
                 chosen[k], part, preferred_element_type=jnp.float32
             )
-        out[:, c * tile : (c + 1) * tile] = mixed.astype(jnp.bfloat16)
+        out[:, c * tile : (c + 1) * tile] = mixed
 
 
 def per_device(tokens, expert_ids, affinity, gate_up, down_proj):
@@ -358,9 +360,9 @@
     dma = pltpu.SemaphoreType.DMA
     vmem = pl.BlockSpec(memory_space=pltpu.VMEM)
     hbm = pl.BlockSpec(memory_space=pl.ANY)
-    return pl.pallas_call(
+    mixed = pl.pallas_call(
         functools.partial(layer_kernel, n, depth, order),
-        out_shape=jax.ShapeDtypeStruct((rows, width), bf16),
+        out_shape=jax.ShapeDtypeStruct((rows, width), jnp.float32),
         in_specs=[vmem, vmem, vmem, hbm, hbm],
         out_specs=vmem,
         scratch_shapes=[
@@ -393,6 +395,7 @@
             collective_id=0, has_side_effects=True, vmem_limit_bytes=60 * 1024 * 1024
         ),
     )(tokens, expert_ids.T, affinity.T, gate_up, down_proj)
+    return mixed.astype(bf16)
 
 
 def solution(mesh):

time: 60.6 us -> 60.9 us (level)
  other arithmetic: 0 us -> 1.87 us
  local copies, waits for them, and re-layouts: 1.73 us -> 0 us
    convert_element_type x0 -> x1, other arithmetic: none -> 1.87 us  [per_device(): return mixed.astype(bf16)]
    unnamed x1 -> x0, local copies, waits for them, and re-layouts: 1.73 us -> none
where the time goes in v7:
time: 60.9 us; the launch traced here: 60.5 us
  Pallas kernels  58.7 us (96%)
  other arithmetic  1.87 us (3%)
    pallas_call x1, Pallas kernels, per_device(): pl.pallas_call(functools.partial(layer_kernel, n, depth, order), out_shap...  58.7 us
    convert_element_type x1, other arithmetic, per_device(): return mixed.astype(bf16)  1.87 us

profile of v7, /device:TPU:0, one launch (start us, length us, event | category | flops | bytes accessed | tf_op | source)
XLA Modules:
  0.0 60.5 jit_solution(9404931804311687036)
XLA Ops:
  0.0 58.7 %shard_map.55 = f32[96,1792]{1,0:T(8,128)} custom-call(bf16[96,1792]{1,0:T(8,128)(2,1)} %tokens.1, s32[2,96]{1,0:T(2,128)} %bitcast.2, f32[2,96]{1,0:T(2,128)} %bitcast.3, bf16[1,1792,2,2048]{3,2,1,0:T(2,128)(2,1)} %gate_up.1, bf16[1,2048,1792]{2,1,0:T(8,128)(2,1)} %down.1), custom_call_target="tpu_custom_call" | custom-call | tf_op jit(solution)/shard_map/pallas_call | solution.py:363
  58.7 1.9 %convert_element_type.3 = bf16[96,1792]{1,0:T(8,128)(2,1)} convert(f32[96,1792]{1,0:T(8,128)} %shard_map.55) | non-fusion elementwise | flops 172032 | bytes 1032192 | tf_op jit(solution)/shard_map/convert_element_type | solution.py:398
